TPU v7x, 256 devices: a whole 4x4x8 slice. The times are simulated.
256 devices in a mesh: row: 32 (over x, y, core), col: 8 (over z).
Axes of the slice: x: 4, y: 4, z: 8, core: 2. Of those that a mesh axis runs over, the one named last changes fastest.
Arguments:
- trailing_in: float32 [2, 32, 256, 8, 8, 256], P(None, 'row', None, None, 'col'), may hold values from 0 to 4, as said below
Outputs:
- factored: float32 [2, 32, 256, 8, 8, 256], P(None, 'row', None, None, 'col')
Inputs may be any that keep to these rules, and one draw needn't show every extreme that they name: `trailing_in`: the matrix is symmetric and positive definite.
All inputs are finite; a program needn't handle non-finite values.
Results may differ from a plain program's by a relative error of at most 0.0003.
Values sent between devices are 32-bit elements; how exact they have to be, the bound alone decides.
A program may use at most 64 MiB of HBM per device.

v0:
```python
import jax
import jax.numpy as jnp
from jax import lax
from jax.sharding import PartitionSpec as P

NB = 256


HIGHEST_PRECISION = lax.Precision.HIGHEST


def from_root(shard, axis, root):
    mine = lax.axis_index(axis) == root
    return lax.psum(jnp.where(mine, shard, jnp.zeros_like(shard)), axis)


def crossing_tiles(panel_rows, row_index, col_index):
    n_row = lax.axis_size("row")
    n_col = lax.axis_size("col")
    groups = n_row // n_col
    slot_index = row_index // n_col
    holder = row_index % n_col == col_index
    chosen = (jnp.arange(groups, dtype=jnp.int32) == slot_index) & holder
    buffer = jnp.where(chosen[None, :, None, None], panel_rows[:, None, :, :], jnp.float32(0.0))
    gathered = lax.psum(buffer, "row")
    return gathered.reshape(panel_rows.shape[0] * groups, NB, NB)


def panel_step(blocks, panel_index, tile_row, tile_col, row_index, col_index):
    n_row = lax.axis_size("row")
    n_col = lax.axis_size("col")
    root_row = panel_index % n_row
    root_col = panel_index % n_col
    local_row = panel_index // n_row
    local_col = panel_index // n_col
    corner = from_root(blocks[local_row, :, local_col, :], "row", root_row)
    factor_diag = jnp.linalg.cholesky(corner)
    column = blocks[:, :, local_col, :]
    flat = column.reshape(column.shape[0] * NB, NB)
    solved = jax.scipy.linalg.solve_triangular(factor_diag, flat.T, lower=True).T.reshape(
        column.shape
    )
    solved = jnp.where(
        (tile_row == panel_index)[:, None, None],
        factor_diag[None],
        jnp.where((tile_row < panel_index)[:, None, None], jnp.float32(0.0), solved),
    )
    panel_rows = from_root(solved, "col", root_col)
    panel_cols = crossing_tiles(panel_rows, row_index, col_index)
    owner = tile_col[local_col] == panel_index
    blocks = blocks.at[:, :, local_col, :].set(jnp.where(owner, solved, column))
    return (blocks, panel_rows, panel_cols)


def trailing(blocks, panel_rows, panel_cols, keep):
    products = jnp.einsum(
        "nho,tuo->nhtu",
        panel_rows,
        panel_cols,
        precision=HIGHEST_PRECISION,
        preferred_element_type=jnp.float32,
    )
    return blocks - jnp.where(keep[None, None, :, None], products, jnp.float32(0.0))


def on_device(trailing_in):
    n_row = lax.axis_size("row")
    n_col = lax.axis_size("col")
    row_index = lax.axis_index("row")
    col_index = lax.axis_index("col")
    loc_rows = trailing_in.shape[0]
    loc_cols = trailing_in.shape[3]
    blocks = trailing_in.reshape(loc_rows, NB, loc_cols, NB)
    tile_row = jnp.arange(loc_rows, dtype=jnp.int32) * n_row + row_index
    tile_col = jnp.arange(loc_cols, dtype=jnp.int32) * n_col + col_index
    keep_zero = tile_col > 0
    keep_one = tile_col > 1
    blocks, rows_zero, cols_zero = panel_step(blocks, 0, tile_row, tile_col, row_index, col_index)
    blocks = trailing(blocks, rows_zero, cols_zero, keep_zero)
    blocks, rows_one, cols_one = panel_step(blocks, 1, tile_row, tile_col, row_index, col_index)
    blocks = trailing(blocks, rows_one, cols_one, keep_one)
    lower_tiles = tile_row[:, None] >= tile_col[None, :]
    blocks = jnp.where(lower_tiles[:, None, :, None], blocks, jnp.float32(0.0))
    return blocks.reshape(loc_rows, 1, NB, loc_cols, 1, NB)


def solution(mesh):
    return jax.shard_map(
        on_device,
        mesh=mesh,
        in_specs=(P(None, "row", None, None, "col", None),),
        out_specs=P(None, "row", None, None, "col", None),
        check_vma=False,
    )
```

profile of v0, /device:TPU:77, one launch (start us, length us, event | category | flops | bytes accessed | tf_op | source)
XLA Modules:
  0.0 790.4 jit_solution(8380969496547220224)
XLA Ops:
  6.5 10.9 %copy.12 = f32[2,1,256,8,1,256]{2,5,3,0,4,1:T(8,128)} copy(f32[2,1,256,8,1,256]{5,4,3,2,1,0:T(1,128)} %param.8) | data formatting | bytes 8388608 | tf_op args[0]
  20.5 109.7 %all-reduce.8.cloned.1.call-done = f32[256,256]{0,1:T(8,128)} async-done(((f32[256,256]{0,1:T(8,128)}), f32[256,256]{0,1:T(8,128)}) %all-reduce.8.cloned.1.call-update) | async-done | bytes 262160 | tf_op jit(solution)/shard_map/psum | solution.py:14
  132.3 11.7 %cholesky.130 = f32[128,128]{1,0:T(8,128)S(1)} custom-call(f32[128,128]{1,0:T(8,128)S(1)} %cholesky.194), custom_call_target="Cholesky" | custom-call | tf_op jit(solution)/shard_map/jit(cholesky)/cholesky | solution.py:37
  144.1 9.8 %custom-call.13 = f32[1,128,128]{1,2,0:T(8,128)S(1)} custom-call(f32[1,128,128]{2,1,0:T(8,128)S(1)} %get-tuple-element.78), custom_call_target="InvertDiagBlocksLowerTriangular" | custom-call | tf_op jit(solution)/shard_map/jit(cholesky)/cholesky | solution.py:37
  154.4 11.7 %cholesky.147 = f32[128,128]{1,0:T(8,128)S(1)} custom-call(f32[128,128]{1,0:T(8,128)S(1)} %convolution_subtract_fusion.3), custom_call_target="Cholesky" | custom-call | tf_op jit(solution)/shard_map/jit(cholesky)/cholesky | solution.py:37
  168.2 4.3 while.6
  172.5 19.7 %custom-call.14 = f32[2,128,128]{1,2,0:T(8,128)S(1)} custom-call(f32[2,128,128]{2,1,0:T(8,128)S(1)} %get-tuple-element.45), custom_call_target="InvertDiagBlocksLowerTriangular" | custom-call | tf_op jit(solution)/shard_map/jit(_solve_triangular)/triangular_solve | solution.py:40
  194.9 70.0 %all-reduce.10.cloned.1.call-done = f32[2,256,256]{2,1,0:T(8,128)} async-done(((f32[2,256,256]{2,1,0:T(8,128)}), f32[2,256,256]{2,1,0:T(8,128)}) %all-reduce.10.cloned.1.call-update) | async-done | bytes 524304 | tf_op jit(solution)/shard_map/psum | solution.py:14
  264.9 2.7 broadcast_select_fusion.1
  268.0 2.0 select_dynamic-update-slice_fusion.1
  270.0 117.3 %all-reduce.12.cloned.1.call-done = f32[8,256,256]{2,1,0:T(8,128)} async-done(((f32[8,256,256]{2,1,0:T(8,128)}), f32[8,256,256]{2,1,0:T(8,128)}) %all-reduce.12.cloned.1.call-update) | async-done | bytes 2097168 | tf_op jit(solution)/shard_map/psum | solution.py:25
  387.3 6.3 select_subtract_fusion
  393.6 2.0 copy-done
  397.9 109.8 %all-reduce.14.cloned.1.call-done = f32[256,256]{0,1:T(8,128)} async-done(((f32[256,256]{0,1:T(8,128)}), f32[256,256]{0,1:T(8,128)}) %all-reduce.14.cloned.1.call-update) | async-done | bytes 262160 | tf_op jit(solution)/shard_map/psum | solution.py:14
  509.8 11.7 %cholesky.164 = f32[128,128]{1,0:T(8,128)S(1)} custom-call(f32[128,128]{1,0:T(8,128)S(1)} %cholesky.197), custom_call_target="Cholesky" | custom-call | tf_op jit(solution)/shard_map/jit(cholesky)/cholesky | solution.py:37
  521.6 9.8 %custom-call.15 = f32[1,128,128]{1,2,0:T(8,128)S(1)} custom-call(f32[1,128,128]{2,1,0:T(8,128)S(1)} %get-tuple-element.74), custom_call_target="InvertDiagBlocksLowerTriangular" | custom-call | tf_op jit(solution)/shard_map/jit(cholesky)/cholesky | solution.py:37
  531.9 11.7 %cholesky.181 = f32[128,128]{1,0:T(8,128)S(1)} custom-call(f32[128,128]{1,0:T(8,128)S(1)} %convolution_subtract_fusion.2), custom_call_target="Cholesky" | custom-call | tf_op jit(solution)/shard_map/jit(cholesky)/cholesky | solution.py:37
  546.3 4.3 while.7
  550.7 19.7 %custom-call.16 = f32[2,128,128]{1,2,0:T(8,128)S(1)} custom-call(f32[2,128,128]{2,1,0:T(8,128)S(1)} %get-tuple-element.46), custom_call_target="InvertDiagBlocksLowerTriangular" | custom-call | tf_op jit(solution)/shard_map/jit(_solve_triangular)/triangular_solve | solution.py:40
  573.0 70.1 %all-reduce.16.cloned.1.call-done = f32[2,256,256]{2,1,0:T(8,128)} async-done(((f32[2,256,256]{2,1,0:T(8,128)}), f32[2,256,256]{2,1,0:T(8,128)}) %all-reduce.16.cloned.1.call-update) | async-done | bytes 524304 | tf_op jit(solution)/shard_map/psum | solution.py:14
  643.1 2.7 broadcast_select_fusion
  648.3 117.1 %all-reduce.18.cloned.1.call-done = f32[8,256,256]{2,1,0:T(8,128)} async-done(((f32[8,256,256]{2,1,0:T(8,128)}), f32[8,256,256]{2,1,0:T(8,128)}) %all-reduce.18.cloned.1.call-update) | async-done | bytes 2097168 | tf_op jit(solution)/shard_map/psum | solution.py:25
  765.4 7.3 select_bitcast_fusion
  772.7 10.9 %copy.27 = f32[2,1,256,8,1,256]{5,4,3,2,1,0:T(1,128)} copy(f32[2,1,256,8,1,256]{2,5,3,0,4,1:T(8,128)} %select_bitcast_fusion) | data formatting | bytes 8388608 | tf_op jit(solution)/shard_map/reshape | solution.py:84
  (85 shorter events, 28.9 us)
Async XLA Ops:
  6.5 123.7 %all-reduce.8.cloned.1.call-start = ((), (), s32[]{:S(2)}) async-start(), calls=%async_computation | async-start | bytes 524288 | tf_op jit(solution)/shard_map/psum | solution.py:14
  19.1 245.8 %all-reduce.10.cloned.1.call-start = ((), (), s32[]{:S(2)}) async-start(), calls=%async_computation.1 | async-start | bytes 1048576 | tf_op jit(solution)/shard_map/psum | solution.py:14
  194.8 192.5 %all-reduce.12.cloned.1.call-start = ((), (), s32[]{:S(2)}) async-start(), calls=%async_computation.2 | async-start | bytes 4194304 | tf_op jit(solution)/shard_map/psum | solution.py:25
  264.9 122.4 %copy-start.1 = (f32[2,256,256]{2,1,0:T(8,128)S(1)}, f32[2,256,256]{2,1,0:T(8,128)}, u32[]{:S(2)}) copy-start(f32[2,256,256]{2,1,0:T(8,128)} %all-reduce.10.cloned.1.call-done) | copy-start | bytes 1572868
  267.6 240.2 %all-reduce.14.cloned.1.call-start = ((), (), s32[]{:S(2)}) async-start(), calls=%async_computation.3 | async-start | bytes 524288 | tf_op jit(solution)/shard_map/psum | solution.py:14
  393.6 2.0 copy-start
  396.4 246.8 %all-reduce.16.cloned.1.call-start = ((), (), s32[]{:S(2)}) async-start(), calls=%async_computation.4 | async-start | bytes 1048576 | tf_op jit(solution)/shard_map/psum | solution.py:14
  573.0 192.4 %all-reduce.18.cloned.1.call-start = ((), (), s32[]{:S(2)}) async-start(), calls=%async_computation.5 | async-start | bytes 4194304 | tf_op jit(solution)/shard_map/psum | solution.py:25
  643.1 122.3 %copy-start.2 = (f32[2,256,256]{2,1,0:T(8,128)S(1)}, f32[2,256,256]{2,1,0:T(8,128)}, u32[]{:S(2)}) copy-start(f32[2,256,256]{2,1,0:T(8,128)} %all-reduce.16.cloned.1.call-done) | copy-start | bytes 1572868
Sparse Core Ops, SparseCore 0:
  19.2 110.9 all-reduce.7
  194.9 69.9 all-reduce.9
  268.2 119.0 all-reduce.11
  396.5 111.2 all-reduce.13
  573.1 69.9 all-reduce.15
  646.2 119.1 all-reduce.17
where the time goes:
time: 796 us; the launch traced here: 790 us
  waiting for transfers between devices  594 us (75%)
  other arithmetic  124 us (16%)
  local copies, waits for them, and re-layouts  37.7 us (5%)
  matrix products  17.3 us (2%)
  between operations  16.5 us (2%)
    psum x4, waiting for transfers between devices, from_root(): return lax.psum(jnp.where(mine, shard, jnp.zeros_like(shard)), axis)  360 us
    psum x2, waiting for transfers between devices, crossing_tiles(): gathered = lax.psum(buffer, 'row')  234 us
    another operation x13, other arithmetic, panel_step(): factor_diag = jnp.linalg.cholesky(corner)  68.7 us
    another operation x5, other arithmetic, panel_step(): jax.scipy.linalg.solve_triangular(factor_diag, flat.T, lower=True)  39.4 us
  transfers between devices with their start and end apart: 6, of which 6 were waited for; matrix products, arithmetic and copies ran while one was open for 1% of the time, Pallas kernels for 0%

commit v1 on v0

v1 whole, which is shorter than its diff:
```python
import jax
import jax.numpy as jnp
from jax import lax
from jax.experimental import pallas as pl
from jax.experimental.pallas import tpu as pltpu
from jax.sharding import PartitionSpec as P

NB = 256
H = 128
F32 = jnp.float32
BF = jnp.bfloat16
HI = lax.Precision.HIGHEST
MESH = pl.DeviceIdType.MESH
NT = (((1,), (1,)), ((), ()))
NN = (((1,), (0,)), ((), ()))
STAGE = (0, 4, 7, 9, 10)


def blk(i, k):
    return STAGE[k] + i - k


def lane_splat(x, j):
    return jnp.broadcast_to(x[:, j:j + 1], (8, H))


def row_splat(x, s):
    return jnp.broadcast_to(x[s:s + 1, :], (8, H))


def tree(xs):
    xs = list(xs)
    while len(xs) > 1:
        xs = [xs[i] + xs[i + 1] if i + 1 < len(xs) else xs[i] for i in range(0, len(xs), 2)]
    return xs[0]


def strip(A, I):
    sub = lax.broadcasted_iota(jnp.int32, (8, H), 0)
    S, T = A[0], I[0]
    cols = [lane_splat(S, j) for j in range(8)]
    D = {(t, j): row_splat(cols[j], t) for j in range(8) for t in range(j, 8)}
    rec, rs, l = [], [], {}
    for s in range(8):
        p = D[s, s]
        r = 1.0 / p
        rec.append(r)
        rs.append(lax.rsqrt(p))
        for t in range(s + 1, 8):
            l[t, s] = D[t, s] * r
        for j in range(s + 1, 8):
            for t in range(j, 8):
                D[t, j] = D[t, j] - l[t, s] * D[j, s]
    u = {}
    for j in range(8):
        for t in range(j + 1, 8):
            acc = -l[t, j]
            for m in range(j + 1, t):
                acc = acc - l[t, m] * u[m, j]
            u[t, j] = acc
    ur = {(t, j): (rec[t] if t == j else u[t, j] * rec[t]) for j in range(8) for t in range(j, 8)}
    dinv = {}
    for i in range(8):
        for j in range(i + 1):
            dinv[i, j] = tree([ur[t, i] if t == j else ur[t, i] * u[t, j] for t in range(i, 8)])
    b0, b1, b2 = (sub & 1) == 1, (sub & 2) == 2, (sub & 4) == 4

    def assemble(v):
        a = [jnp.where(b0, v[2 * i + 1], v[2 * i]) for i in range(4)]
        b = [jnp.where(b1, a[2 * i + 1], a[2 * i]) for i in range(2)]
        return jnp.where(b2, b[1], b[0])

    zero = jnp.zeros((8, H), F32)
    one = jnp.ones((8, H), F32)
    srow = [row_splat(S, s) for s in range(8)]
    trow = [row_splat(T, s) for s in range(8)]
    dcol = [assemble([dinv[max(t, s), min(t, s)] for t in range(8)]) for s in range(8)]
    Z = tree([dcol[s] * srow[s] for s in range(8)])
    ZT = tree([dcol[s] * trow[s] for s in range(8)])
    ucol = [assemble([zero if t < s else (one if t == s else u[t, s]) for t in range(8)]) for s in range(8)]
    out = assemble(rs) * tree([ucol[s] * trow[s] for s in range(8)])
    zrow = [row_splat(Z, s) for s in range(8)]
    ztrow = [row_splat(ZT, s) for s in range(8)]
    An, In = [], []
    for g in range(1, len(A)):
        a = [lane_splat(A[g], s) for s in range(8)]
        An.append(pltpu.roll(A[g] - tree([a[s] * zrow[s] for s in range(8)]), H - 8, 1))
        In.append(I[g] - tree([a[s] * ztrow[s] for s in range(8)]))
    An.append(zero)
    In.append(zero)
    return An, In, out


def chol_inv(a, out_ref):
    sub = lax.broadcasted_iota(jnp.int32, (8, H), 0)
    lane = lax.broadcasted_iota(jnp.int32, (8, H), 1)
    A = [a[8 * g:8 * g + 8, :] for g in range(16)]
    I = [jnp.where(lane == sub + 8 * g, 1.0, 0.0).astype(F32) for g in range(16)]

    def body(k, c):
        An, In, out = strip(list(c[:16]), list(c[16:]))
        out_ref[pl.ds(pl.multiple_of(8 * k, 8), 8), :] = out
        return tuple(An) + tuple(In)

    lax.fori_loop(0, 16, body, tuple(A) + tuple(I))


def split(a):
    h = a.astype(BF)
    return h, (a - h.astype(F32)).astype(BF)


def dot3(a, b, dims):
    def g(p, q):
        return lax.dot_general(p, q, dims, preferred_element_type=F32)
    return g(a[0], b[0]) + (g(a[0], b[1]) + g(a[1], b[0]))


def dot_hi(a, b):
    return lax.dot_general(a, b, NT, precision=HI, preferred_element_type=F32)


def kernel(x, o, tiles, cols, rows, corner, fac, cm, prow, phi, plo, cthi, ctlo,
           ld, ldc, ldr, st, colsem, rowsem, csem, fsem, s1, s2, s3, s4, sr, sc, fz, fx, fy, fk):
    r = lax.axis_index("row")
    z = lax.axis_index("col")
    px, py, k = r // 8, (r // 2) % 4, r % 2
    u = jnp.where(k == 0, px, py)
    v = jnp.where(k == 0, py, px)

    def plane(uu, vv):
        xx = jnp.where(k == 0, uu, vv)
        yy = jnp.where(k == 0, vv, uu)
        return (xx * 8 + yy * 2 + k, z)

    partner = (r + 1 - 2 * k, z)
    root = (r == 0) & (z == 0)

    def load(a, b, h):
        return pltpu.make_async_copy(x.at[a, :, b, h, :], tiles.at[a, b, :, pl.ds(h * H, H)], ld.at[a, b, h])

    def load_col(b, h):
        return pltpu.make_async_copy(x.at[0, :, b, h, :], cols.at[k, b, :, pl.ds(h * H, H)], ldc.at[b, h])

    def load_row(a, h):
        return pltpu.make_async_copy(x.at[a, :, 0, h, :], rows.at[z, a, :, pl.ds(h * H, H)], ldr.at[a, h])

    @pl.when(z < 2)
    def _():
        for a in range(2):
            for h in range(2):
                load_row(a, h).start()

    @pl.when(r < 2)
    def _():
        for b in (2, 3, 4, 5, 6, 7, 0, 1):
            for h in range(2):
                load_col(b, h).start()

    for a in range(2):
        for b in range(8):
            for h in range(2):
                load(a, b, h).start()

    barrier = pltpu.get_barrier_semaphore()

    def greet(dev):
        pl.semaphore_signal(barrier, inc=1, device_id=dev, device_id_type=MESH)

    for d in range(1, 4):
        greet((((px + d) % 4) * 8 + py * 2 + k, z))
        greet((px * 8 + ((py + d) % 4) * 2 + k, z))
    greet(partner)
    for d in range(1, 8):
        greet((r, (z + d) % 8))

    extra = (r == 1) & (z == 1)

    @pl.when(extra)
    def _():
        greet((0, 0))

    @pl.when(root)
    def _():
        greet((1, 1))

    pl.semaphore_wait(barrier, jnp.where(root | extra, 15, 14))

    def send(src, dst, ss, rs, dev):
        return pltpu.make_async_remote_copy(src_ref=src, dst_ref=dst, send_sem=ss, recv_sem=rs, device_id=dev, device_id_type=MESH)

    def corner_send(i, dev):
        return send(rows.at[i, 0], corner.at[i], sc.at[0], csem.at[i], dev)

    def row_send(p, a, n, ds):
        zz = (z + (8 - ds if p == 0 else ds)) % 8
        return send(rows.at[p, a], rows.at[p, a], sr.at[p, n, a], rowsem.at[p, a], (r, zz))

    pos = [(8 - z) % 8, (z + 7) % 8]
    hops = {0: (3, 1, 7), 3: (2, 1, 7), 5: (1,)}

    def row_wait(p, a):
        send(rows.at[p, a], rows.at[p, a], sr.at[p, 0, a], rowsem.at[p, a], (r, z)).wait_recv()

    def col_send(q, n, e, b, dev):
        return send(cols.at[k, b], cols.at[k, b], q.at[n, e], colsem.at[k, b], dev)

    def col_wait(kk, b):
        send(cols.at[kk, b], cols.at[kk, b], s4.at[b], colsem.at[kk, b], partner).wait_recv()

    def give(b):
        return send(cols.at[k, b], cols.at[k, b], s4.at[b], colsem.at[k, b], partner)

    def level1(n, e):
        vv = (2, 1, 3)[n]
        return col_send(s1, n, e, 2 * vv + e, plane(0, vv))

    def level2(n, e):
        return col_send(s2, n, e, 2 * v + e, plane((2, 1, 3)[n], v))

    def level3(n, e):
        return col_send(s3, n, e, 2 * v + e, plane(u, (v + (2, 1, 3)[n]) % 4))

    def back(n):
        return (u == 0) & ((v + (2, 1, 3)[n]) % 4 == 0)

    src = r < 2

    @pl.when(z < 2)
    def _():
        for a in range(2):
            for h in range(2):
                load_row(a, h).wait()

    @pl.when((r == 1) & (z == 0))
    def _():
        corner_send(0, (0, 0)).start()

    @pl.when(extra)
    def _():
        corner_send(1, (0, 0)).start()

    for p in range(2):
        @pl.when(z == p)
        def _():
            for n in range(3):
                for a in range(2):
                    row_send(p, a, n, hops[0][n]).start()

    @pl.when(src)
    def _():
        for b in (2, 3, 4, 5, 6, 7, 0, 1):
            for h in range(2):
                load_col(b, h).wait()
        for e in range(2):
            for n in range(3):
                level1(n, e).start()
        for e in range(2):
            for n in range(3):
                level2(n, e).start()
        for e in range(2):
            for n in range(3):
                @pl.when(jnp.logical_not(back(n)))
                def _():
                    level3(n, e).start()
        for b in range(8):
            give(b).start()

    @pl.when((u == 0) & (v > 0))
    def _():
        for e in range(2):
            col_wait(k, 2 * v + e)
            for n in range(3):
                level2(n, e).start()
            for n in range(3):
                @pl.when(jnp.logical_not(back(n)))
                def _():
                    level3(n, e).start()
            give(2 * v + e).start()

    def row_forward(at):
        for p in range(2):
            @pl.when(pos[p] == at)
            def _():
                for a in range(2):
                    row_wait(p, a)
                    for n in range(len(hops[at])):
                        row_send(p, a, n, hops[at][n]).start()

    def stage_ref(s):
        return fac.at[pl.ds(STAGE[s], STAGE[s + 1] - STAGE[s])]

    def fac_send(s, ss, dev):
        return send(stage_ref(s), stage_ref(s), ss, fsem.at[s], dev)

    @pl.when(root)
    def _():
        for i in range(2):
            for j in range(i + 1):
                cm[i, j] = rows[0, 0, i * H:(i + 1) * H, j * H:(j + 1) * H]
        for s in range(4):
            chol_inv(cm[s, s], fac.at[blk(s, s)])
            if s == 0:
                send(rows.at[0, 0], corner.at[0], sc.at[0], csem.at[0], (r, z)).wait_recv()
                for i in range(2):
                    for j in range(2):
                        cm[2 + i, j] = corner[0, i * H:(i + 1) * H, j * H:(j + 1) * H]
                send(rows.at[0, 0], corner.at[1], sc.at[0], csem.at[1], (r, z)).wait_recv()
                for i in range(2):
                    for j in range(i + 1):
                        cm[2 + i, 2 + j] = corner[1, i * H:(i + 1) * H, j * H:(j + 1) * H]
            for i in range(s + 1, 4):
                fac[blk(i, s)] = dot_hi(cm[i, s], fac[blk(s, s)])
            for d in (4, 3, 5, 2, 6, 1, 7):
                fac_send(s, fz.at[s, d - 1], (0, d)).start()
            for n in range(3):
                fac_send(s, fx.at[s, n], ((2, 1, 3)[n] * 8, z)).start()
            for n in range(3):
                fac_send(s, fy.at[s, n], ((2, 1, 3)[n] * 2, z)).start()
            fac_send(s, fk.at[s], partner).start()
            for i in range(s + 1, 4):
                for j in range(s + 1, i + 1):
                    cm[i, j] = cm[i, j] - dot_hi(fac[blk(i, s)], fac[blk(j, s)])

    row_forward(3)

    @pl.when(u > 0)
    def _():
        for e in range(2):
            col_wait(k, 2 * v + e)
            for n in range(3):
                level3(n, e).start()
            give(2 * v + e).start()

    row_forward(5)

    @pl.when(jnp.logical_not(src))
    def _():
        for n in (1, 2, 0):
            for e in range(2):
                b = 2 * ((v + (2, 1, 3)[n]) % 4) + e
                col_wait(k, b)
                give(b).start()

    def store(a, b, h):
        return pltpu.make_async_copy(tiles.at[a, b, :, pl.ds(h * H, H)], o.at[a, :, b, h, :], st.at[a, b, h])

    def wait_loads(t, c):
        for h in range(2):
            load(t // 8, t % 8, h).wait()

        @pl.when(r + 32 * (t // 8) < z + 8 * (t % 8))
        def _():
            tiles[t // 8, t % 8] = jnp.zeros((NB, NB), F32)
            for h in range(2):
                store(t // 8, t % 8, h).start()
        return c

    lax.fori_loop(0, 16, wait_loads, 0)

    def fac_arrive(s):
        @pl.when(jnp.logical_not(root))
        def _():
            fac_send(s, fk.at[s], partner).wait_recv()

            @pl.when((px == 0) & (py == 0) & (k == 0))
            def _():
                for n in range(3):
                    fac_send(s, fx.at[s, n], ((2, 1, 3)[n] * 8, z)).start()

            @pl.when((py == 0) & (k == 0))
            def _():
                for n in range(3):
                    fac_send(s, fy.at[s, n], (px * 8 + (2, 1, 3)[n] * 2, z)).start()

            @pl.when(k == 0)
            def _():
                fac_send(s, fk.at[s], partner).start()

    def solve(s):
        w = (s % 2) * H
        fs = {m: split(fac[blk(s, m)]) for m in range(s + 1)}
        at = slice(s * H, (s + 1) * H)
        for a in range(2):
            t = rows[s // 2, a, :, w:w + H]
            for m in range(s):
                ms = slice(m * H, (m + 1) * H)
                t = t - dot3((phi[a, :, ms], plo[a, :, ms]), fs[m], NT)
            t = dot3(split(t), fs[s], NT)
            prow[a, :, at] = t
            phi[a, :, at], plo[a, :, at] = split(t)

        def col(b, c):
            @pl.when(z + 8 * b <= r + 32)
            def _():
                t = cols[s // 2, b, w:w + H, :]
                for m in range(s):
                    ms = slice(m * H, (m + 1) * H)
                    t = t - dot3(fs[m], (cthi[b, ms, :], ctlo[b, ms, :]), NN)
                t = dot3(fs[s], split(t), NN)
                cthi[b, at, :], ctlo[b, at, :] = split(t)
            return c

        lax.fori_loop(0, 8, col, 0)

    def update(p, last):
        at = slice(p * NB, (p + 1) * NB)

        def tile(t, c):
            a, b = t // 8, t % 8

            @pl.when((r + 32 * a >= z + 8 * b) & (z + 8 * b >= 2))
            def _():
                d = dot3((phi[a, :, at], plo[a, :, at]), (cthi[b, at, :], ctlo[b, at, :]), NN)
                tiles[a, b] = tiles[a, b] - d
                if last:
                    for h in range(2):
                        store(a, b, h).start()
            return c

        lax.fori_loop(0, 16, tile, 0)

    for s in range(4):
        fac_arrive(s)
        if s % 2 == 0:
            p = s // 2
            for a in range(2):
                if p == 0:
                    @pl.when((z != 0) & (pos[0] != 3) & (pos[0] != 5))
                    def _():
                        row_wait(0, a)
                else:
                    @pl.when((z != 1) & (pos[1] != 3) & (pos[1] != 5))
                    def _():
                        row_wait(1, a)

            @pl.when(k != p)
            def _():
                for b in range(8):
                    col_wait(p, b)
        solve(s)
        if s == 1:
            update(0, False)

    for p in range(2):
        @pl.when(z == p)
        def _():
            for a in range(2):
                @pl.when((r + 32 * a >= p))
                def _():
                    t = prow[a, :, p * NB:(p + 1) * NB]
                    ri = lax.broadcasted_iota(jnp.int32, (NB, NB), 0)
                    ci = lax.broadcasted_iota(jnp.int32, (NB, NB), 1)
                    keep = (ri >= ci) | (r + 32 * a > p)
                    tiles[a, 0] = jnp.where(keep, t, 0.0)
                    for h in range(2):
                        store(a, 0, h).start()

    update(1, True)

    @pl.when((r == 1) & (z == 0))
    def _():
        corner_send(0, (0, 0)).wait_send()

    @pl.when(extra)
    def _():
        corner_send(1, (0, 0)).wait_send()

    for p in range(2):
        for at in (0, 3, 5):
            @pl.when(pos[p] == at)
            def _():
                for n in range(len(hops[at])):
                    for a in range(2):
                        row_send(p, a, n, hops[at][n]).wait_send()
    for e in range(2):
        for n in range(3):
            @pl.when(src)
            def _():
                level1(n, e).wait_send()

            @pl.when(u == 0)
            def _():
                level2(n, e).wait_send()

            @pl.when(jnp.logical_not(back(n)))
            def _():
                level3(n, e).wait_send()
    for b in range(8):
        give(b).wait_send()
    for s in range(4):
        @pl.when(root)
        def _():
            for d in range(1, 8):
                fac_send(s, fz.at[s, d - 1], (0, d)).wait_send()

        @pl.when((px == 0) & (py == 0) & (k == 0))
        def _():
            for n in range(3):
                fac_send(s, fx.at[s, n], ((2, 1, 3)[n] * 8, z)).wait_send()

        @pl.when((py == 0) & (k == 0))
        def _():
            for n in range(3):
                fac_send(s, fy.at[s, n], (px * 8 + (2, 1, 3)[n] * 2, z)).wait_send()

        @pl.when(k == 0)
        def _():
            fac_send(s, fk.at[s], partner).wait_send()

    def drain(t, c):
        for h in range(2):
            store(t // 8, t % 8, h).wait()
        return c

    lax.fori_loop(0, 16, drain, 0)


def on_device(trailing_in):
    x = trailing_in.reshape(2, NB, 8, 2, H)
    dma = pltpu.SemaphoreType.DMA
    out = pl.pallas_call(
        kernel,
        out_shape=jax.ShapeDtypeStruct(x.shape, F32),
        in_specs=[pl.BlockSpec(memory_space=pl.ANY)],
        out_specs=pl.BlockSpec(memory_space=pl.ANY),
        scratch_shapes=[
            pltpu.VMEM((2, 8, NB, NB), F32),
            pltpu.VMEM((2, 8, NB, NB), F32),
            pltpu.VMEM((2, 2, NB, NB), F32),
            pltpu.VMEM((2, NB, NB), F32),
            pltpu.VMEM((10, H, H), F32),
            pltpu.VMEM((4, 4, H, H), F32),
            pltpu.VMEM((2, NB, 2 * NB), F32),
            pltpu.VMEM((2, NB, 2 * NB), BF),
            pltpu.VMEM((2, NB, 2 * NB), BF),
            pltpu.VMEM((8, 2 * NB, NB), BF),
            pltpu.VMEM((8, 2 * NB, NB), BF),
            dma((2, 8, 2)), dma((8, 2)), dma((2, 2)), dma((2, 8, 2)),
            dma((2, 8)), dma((2, 2)), dma((2,)), dma((4,)),
            dma((3, 2)), dma((3, 2)), dma((3, 2)), dma((8,)),
            dma((2, 3, 2)), dma((1,)), dma((4, 7)), dma((4, 3)), dma((4, 3)), dma((4,)),
        ],
        compiler_params=pltpu.CompilerParams(
            collective_id=0, has_side_effects=True, vmem_limit_bytes=56 << 20
        ),
    )(x)
    return out.reshape(trailing_in.shape)


def solution(mesh):
    spec = P(None, "row", None, None, "col", None)
    return jax.shard_map(on_device, mesh=mesh, in_specs=(spec,), out_specs=spec, check_vma=False)
```

time: 796 us -> 91.9 us (0.12)
  the two profiles are of different devices: /device:TPU:77 before, /device:TPU:15 now
where the time goes in v1:
time: 91.9 us; the launch traced here: 91.8 us
  Pallas kernels  84.7 us (92%)
  local copies, waits for them, and re-layouts  7.08 us (8%)
    pallas_call x1, Pallas kernels, on_device(): pl.pallas_call(kernel, out_shape=jax.ShapeDtypeStruct(x.shape, F32), in_s...  84.7 us
    unnamed x1, local copies, waits for them, and re-layouts  7.08 us

profile of v1, /device:TPU:15, one launch (start us, length us, event | category | flops | bytes accessed | tf_op | source)
XLA Modules:
  0.0 91.8 jit_solution(2951612971391680860)
XLA Ops:
  0.0 84.7 %shard_map.17 = f32[2,256,8,2,128]{4,3,2,1,0:T(2,128)} custom-call(f32[2,256,8,2,128]{4,3,2,1,0:T(2,128)} %bitcast.3), custom_call_target="tpu_custom_call" | custom-call | tf_op jit(solution)/shard_map/pallas_call | solution.py:522
  84.7 7.1 %copy.4 = f32[2,1,256,8,1,256]{5,4,3,2,1,0:T(1,128)} copy(f32[2,1,256,8,1,256]{5,4,3,2,1,0:T(1,128)} %bitcast.2) | data formatting | bytes 8388608

commit v2 on v0

v2 whole, which is shorter than its diff:
```python
import jax
import jax.numpy as jnp
from jax import lax
from jax.experimental import pallas as pl
from jax.experimental.pallas import tpu as pltpu
from jax.sharding import PartitionSpec as P

NB = 256
H = 128
F32 = jnp.float32
BF = jnp.bfloat16
HI = lax.Precision.HIGHEST
MESH = pl.DeviceIdType.MESH
NT = (((1,), (1,)), ((), ()))
NN = (((1,), (0,)), ((), ()))
STAGE = (0, 4, 7, 9, 10)


def blk(i, k):
    return STAGE[k] + i - k


def lane_splat(x, j):
    return jnp.broadcast_to(x[:, j:j + 1], (8, H))


def row_splat(x, s):
    return jnp.broadcast_to(x[s:s + 1, :], (8, H))


def tree(xs):
    xs = list(xs)
    while len(xs) > 1:
        xs = [xs[i] + xs[i + 1] if i + 1 < len(xs) else xs[i] for i in range(0, len(xs), 2)]
    return xs[0]


def assemble(v, sub):
    b0, b1, b2 = (sub & 1) == 1, (sub & 2) == 2, (sub & 4) == 4
    a = [v[2 * i] if v[2*i] is v[2*i+1] else jnp.where(b0, v[2 * i + 1], v[2 * i]) for i in range(4)]
    b = [a[2 * i] if a[2*i] is a[2*i+1] else jnp.where(b1, a[2 * i + 1], a[2 * i]) for i in range(2)]
    return b[0] if b[0] is b[1] else jnp.where(b2, b[1], b[0])


def chol_inv(a, out_ref, n=16):
    sub = lax.broadcasted_iota(jnp.int32, (8, H), 0)
    lane = lax.broadcasted_iota(jnp.int32, (8, H), 1)
    zero = jnp.zeros((8, H), F32)
    one = jnp.ones((8, H), F32)
    A = [a[8 * g:8 * g + 8, :] for g in range(n)]
    I = [jnp.where(lane == sub + 8 * g, 1.0, 0.0).astype(F32) for g in range(n)]
    c = [lane_splat(A[0], j) for j in range(8)]
    for k in range(n):
        w = 8 * k
        more = k + 1 < n
        if more:
            a1 = [lane_splat(A[k + 1], w + s) for s in range(8)]
            cn = [lane_splat(A[k + 1], w + 8 + j) for j in range(8)]
        D = {(t, j): row_splat(c[j], t) for j in range(8) for t in range(j, 8)}
        rec, rs, l = [], [], {}
        for s in range(8):
            p = D[s, s]
            r = 1.0 / p
            rec.append(r)
            rs.append(lax.rsqrt(p))
            for t in range(s + 1, 8):
                l[t, s] = D[t, s] * r
            for j in range(s + 1, 8):
                for t in range(j, 8):
                    D[t, j] = D[t, j] - l[t, s] * D[j, s]
            if more:
                x = a1[s]
                m = x * r
                for j in range(8):
                    cn[j] = cn[j] - m * row_splat(x, j)
                for t in range(s + 1, 8):
                    a1[t] = a1[t] - x * l[t, s]
        u = {}
        for j in range(8):
            for t in range(j + 1, 8):
                u[t, j] = -tree([l[t, j]] + [l[t, m] * u[m, j] for m in range(j + 1, t)])
        S, T = A[k], I[k]
        ucol = [assemble([zero if t < s else (one if t == s else u[t, s]) for t in range(8)], sub) for s in range(8)]
        T1 = tree([ucol[s] * row_splat(T, s) for s in range(8)])
        out_ref[w:w + 8, :] = assemble(rs, sub) * T1
        if more:
            recv = assemble(rec, sub)
            S1 = tree([ucol[s] * row_splat(S, s) for s in range(8)]) * recv
            T2 = T1 * recv
            vcol = [assemble([u[t, s] if s < t else (one if s == t else zero) for s in range(8)], sub) for t in range(8)]
            Z = tree([vcol[t] * row_splat(S1, t) for t in range(8)])
            ZT = tree([vcol[t] * row_splat(T2, t) for t in range(8)])
            zrow = [row_splat(Z, s) for s in range(8)]
            ztrow = [row_splat(ZT, s) for s in range(8)]
            for g in range(k + 1, n):
                ag = [lane_splat(A[g], w + s) for s in range(8)]
                A[g] = A[g] - tree([ag[s] * zrow[s] for s in range(8)])
                I[g] = I[g] - tree([ag[s] * ztrow[s] for s in range(8)])
            c = cn


def split(a):
    h = a.astype(BF)
    return h, (a - h.astype(F32)).astype(BF)


def dot3(a, b, dims):
    def g(p, q):
        return lax.dot_general(p, q, dims, preferred_element_type=F32)
    return g(a[0], b[0]) + (g(a[0], b[1]) + g(a[1], b[0]))


def dot_hi(a, b):
    return lax.dot_general(a, b, NT, precision=HI, preferred_element_type=F32)


CH = 64
NC = 2 * NB // CH
PER = NB // CH
HOP = 4
DIRS = ((1, 0), (0, 1), (-1, 0), (0, -1))
PARENT = {(1, 0): 0, (2, 0): 0, (1, 1): 1, (1, 3): 3, (2, 1): 0, (1, 2): 1, (0, 1): 2, (0, 3): 2,
          (3, 0): 0, (2, 3): 3, (2, 2): 0, (0, 2): 2, (3, 1): 0, (3, 3): 0, (3, 2): 0}
FSTEP = (7, 10, 13, 16)
FLEVEL = 3
STEPS = NC + 5 * HOP
OTHER = (2, 1, 3)
ZFAN = {0: (2, 6, 1, 7), 2: (4, 3), 6: (5,)}


def tree_tables():
    depth = {(0, 0): 0}
    kids = {v: [] for v in list(PARENT) + [(0, 0)]}
    for v, d in PARENT.items():
        kids[(v[0] - DIRS[d][0]) % 4, (v[1] - DIRS[d][1]) % 4].append(d)
    while len(depth) < 16:
        for v, d in PARENT.items():
            up = ((v[0] - DIRS[d][0]) % 4, (v[1] - DIRS[d][1]) % 4)
            if up in depth:
                depth[v] = depth[up] + 1
    child = [sum(1 << (4 * v[0] + v[1]) for v in kids if d in kids[v]) for d in range(4)]
    bits = [sum(1 << (4 * v[0] + v[1]) for v in depth if depth[v] >> n & 1) for n in range(3)]
    return child, bits


CHILD, DEPTH = tree_tables()


def bit(mask, n):
    hit = False
    for i in range(16):
        if mask >> i & 1:
            hit = (n == i) | hit
    return hit


def kernel(x, tiles, cols, rows, corner, fac, cm, linv, phi, plo, cthi, ctlo,
           ld, ldc, ldr, colsem, givesem, rowsem, csem, fsem, scol, sgive, srow, sc, fz, fx, fy, fk):
    r = lax.axis_index("row")
    z = lax.axis_index("col")
    px, py, k = r // 8, (r // 2) % 4, r % 2
    partner = (r + 1 - 2 * k, z)
    root = (r == 0) & (z == 0)
    src = r < 2
    extra = (r == 1) & (z == 1)

    def load(a, b, h):
        return pltpu.make_async_copy(x.at[a, :, b, h, :], tiles.at[a, b, :, pl.ds(h * H, H)], ld.at[a, b, h])

    def load_col(b, h):
        return pltpu.make_async_copy(x.at[0, :, b, h, :], cols.at[k, b, :, pl.ds(h * H, H)], ldc.at[b, h])

    def load_row(a, h):
        return pltpu.make_async_copy(x.at[a, :, 0, h, :], rows.at[z, a, :, pl.ds(h * H, H)], ldr.at[a, h])

    @pl.when(z < 2)
    def _():
        for a in range(2):
            for h in range(2):
                load_row(a, h).start()

    @pl.when(src)
    def _():
        for b in range(8):
            for h in range(2):
                load_col(b, h).start()

    for a in range(2):
        for b in range(8):
            for h in range(2):
                load(a, b, h).start()

    barrier = pltpu.get_barrier_semaphore()

    def greet(dev):
        pl.semaphore_signal(barrier, inc=1, device_id=dev, device_id_type=MESH)

    for d in (1, 3):
        greet((((px + d) % 4) * 8 + py * 2 + k, z))
        greet((px * 8 + ((py + d) % 4) * 2 + k, z))
    greet(partner)
    for d in (1, 7):
        greet((r, (z + d) % 8))

    @pl.when(k == 0)
    def _():
        greet((((px + 2) % 4) * 8 + py * 2, z))
        greet((px * 8 + ((py + 2) % 4) * 2, z))

    @pl.when(r == 0)
    def _():
        for d in (2, 6):
            greet((0, (z + d) % 8))

    @pl.when(extra)
    def _():
        greet((0, 0))

    @pl.when(root)
    def _():
        greet((1, 1))

    @pl.when(z < 2)
    def _():
        for a in range(2):
            for h in range(2):
                load_row(a, h).wait()

    @pl.when(root)
    def _():
        for i in range(2):
            for j in range(i + 1):
                cm[i, j] = rows[0, 0, i * H:(i + 1) * H, j * H:(j + 1) * H]
        chol_inv(cm[0, 0], linv)

    peers = 7 + jnp.where(k == 0, 2, 0) + jnp.where(r == 0, 2, 0) + jnp.where(root | extra, 1, 0)
    pl.semaphore_wait(barrier, peers)

    def send(ref, ss, rs, dev, to=None):
        return pltpu.make_async_remote_copy(
            src_ref=ref, dst_ref=ref if to is None else to, send_sem=ss, recv_sem=rs, device_id=dev, device_id_type=MESH)

    def start(c):
        c.start()

    def wait_send(c):
        c.wait_send()

    def corner_send(i, dev):
        return send(rows.at[i, 0], sc.at[0], csem.at[i], dev, corner.at[i])

    def row_send(p, i, d, zz):
        ref = rows.at[p, i // PER, pl.ds((i % PER) * CH, CH)]
        return send(ref, srow.at[p, d, i], rowsem.at[p, i], (r, zz))

    row_depth = (jnp.where(z < 3, z, 8 - z),
                 jnp.where(z == 0, 1, jnp.where((z == 7) & (r > 0), 2, z - 1)))
    row_down = ((z == 0) | (z > 3), (z == 1) | ((z == 0) & (r > 0)))
    row_up = (z < 2, (z > 0) & ((z < 6) | ((z == 6) & (r == 0))))
    row_from = (z > 0, z != 1)
    row_first = (jnp.where(r == 0, PER, 0), jnp.where(r < 2, PER, 0))

    def row_spread(p, i, act):
        @pl.when(row_down[p])
        def _():
            act(row_send(p, i, 0, (z + 7) % 8))

        @pl.when(row_up[p])
        def _():
            act(row_send(p, i, 1, (z + 1) % 8))

    def row_step(p, step):
        i = step - row_depth[p] * HOP

        @pl.when((i >= row_first[p]) & (i < NC) & (row_down[p] | row_up[p]))
        def _():
            @pl.when(row_from[p])
            def _():
                row_send(p, i, 0, z).wait_recv()
            row_spread(p, i, start)

    frames, links = [], []
    fx_, fy_ = px, py
    for t in range(4):
        n = fx_ * 4 + fy_
        frames.append((bit(DEPTH[0], n).astype(jnp.int32) + 2 * bit(DEPTH[1], n).astype(jnp.int32)
                       + 4 * bit(DEPTH[2], n).astype(jnp.int32)) * HOP)
        links.append([bit(CHILD[d], n) for d in range(4)])
        fx_, fy_ = fy_, (4 - fx_) % 4

    def col_send(t, i, d, dev):
        ref = cols.at[k, t + 4 * (i // PER), pl.ds((i % PER) * CH, CH)]
        return send(ref, scol.at[t, d, i], colsem.at[t, i], dev)

    def col_spread(t, i, act):
        for d in range(4):
            dx, dy = DIRS[(d + t) % 4]

            @pl.when(links[t][d])
            def _():
                act(col_send(t, i, d, (((px + dx + 4) % 4) * 8 + ((py + dy + 4) % 4) * 2 + k, z)))

    def give(b):
        return send(cols.at[k, b], sgive.at[b], givesem.at[b], partner)

    def col_step(t, step):
        i = step - frames[t]

        @pl.when((i >= 0) & (i < NC))
        def _():
            @pl.when(jnp.logical_not(src))
            def _():
                col_send(t, i, 0, partner).wait_recv()
            col_spread(t, i, start)

            @pl.when(i % PER == PER - 1)
            def _():
                give(t + 4 * (i // PER)).start()

    def use(b):
        return px >= b - 4

    def fac_send(s, ss, dev):
        ref = fac.at[pl.ds(STAGE[s], STAGE[s + 1] - STAGE[s])]
        return send(ref, ss, fsem.at[s], dev)

    def fac_spread(s, act):
        for at, to in ZFAN.items():
            @pl.when((r == 0) & (z == at))
            def _():
                for d in to:
                    act(fac_send(s, fz.at[s, d - 1], (0, d)))

        @pl.when(r == 0)
        def _():
            for n in range(3):
                act(fac_send(s, fx.at[s, n], (OTHER[n] * 8, z)))

        @pl.when((py == 0) & (k == 0))
        def _():
            for n in range(3):
                act(fac_send(s, fy.at[s, n], (px * 8 + OTHER[n] * 2, z)))

        @pl.when(k == 0)
        def _():
            act(fac_send(s, fk.at[s], partner))

    def fac_wait(s):
        fac_send(s, fk.at[s], partner).wait_recv()

    relay = (k == 0) & (py == 0) & jnp.logical_not(root)
    level = (jnp.where((z > 2) & (z < 6), 1, 0) + jnp.where(px > 0, 1, 0)) * FLEVEL

    @pl.when((r == 1) & (z == 0))
    def _():
        corner_send(0, (0, 0)).start()

    @pl.when(extra)
    def _():
        corner_send(1, (0, 0)).start()

    @pl.when(src)
    def _():
        for b in range(8):
            for h in range(2):
                load_col(b, h).wait()

    def step_body(step, c):
        for p in range(2):
            row_step(p, step)
        for t in range(4):
            col_step(t, step)
        for s in range(4):
            @pl.when(relay & (step == FSTEP[s] + level))
            def _():
                fac_wait(s)
                fac_spread(s, start)
        return c

    lax.fori_loop(0, jnp.where(root, NC, jnp.where((r == 0) & (z > 5), STEPS + HOP, STEPS)), step_body, 0)

    @pl.when(root)
    def _():
        for i in range(2):
            send(rows.at[0, 0], sc.at[0], csem.at[i], partner, corner.at[i]).wait_recv()
        for i in range(2):
            for j in range(2):
                cm[2 + i, j] = corner[0, i * H:(i + 1) * H, j * H:(j + 1) * H]
            for j in range(i + 1):
                cm[2 + i, 2 + j] = corner[1, i * H:(i + 1) * H, j * H:(j + 1) * H]

        def stage(t, c):
            @pl.when(t > 0)
            def _():
                chol_inv(cm[t, t], linv)
            for s in range(4):
                @pl.when(t == s)
                def _():
                    fac[blk(s, s)] = linv[...]
                    for i in range(s + 1, 4):
                        fac[blk(i, s)] = dot_hi(cm[i, s], linv[...])
                    fac_spread(s, start)
                    for i in range(s + 1, 4):
                        for j in range(s + 1, i + 1):
                            cm[i, j] = cm[i, j] - dot_hi(fac[blk(i, s)], fac[blk(j, s)])
            return c

        lax.fori_loop(0, 4, stage, 0)

    for p in range(2):
        @pl.when(row_from[p] & jnp.logical_not(row_down[p] | row_up[p]))
        def _():
            def body(i, c):
                row_send(p, i, 0, z).wait_recv()
                return c
            lax.fori_loop(row_first[p], NC, body, 0)

    for b in range(8):
        give(b).wait_recv()

    for a in range(2):
        for b in range(8):
            for h in range(2):
                load(a, b, h).wait()

    def solve(s):
        w = (s % 2) * H
        at = slice(s * H, (s + 1) * H)
        done = slice(0, s * H)
        fs = split(fac[blk(s, s)])
        if s:
            fl = split(jnp.concatenate([fac[blk(s, m)] for m in range(s)], axis=1))
        for a in range(2):
            t = rows[s // 2, a, :, w:w + H]
            if s:
                t = t - dot3((phi[a, :, done], plo[a, :, done]), fl, NT)
            t = dot3(split(t), fs, NT)
            phi[a, :, at], plo[a, :, at] = split(t)

            @pl.when((z == s // 2) & (r + 32 * a >= z))
            def _():
                if w == 0:
                    tiles[a, 0, :, H:] = jnp.zeros((NB, H), F32)
                tiles[a, 0, :, w:w + H] = t

        def col(b):
            t = cols[s // 2, b, w:w + H, :]
            if s:
                t = t - dot3(fl, (cthi[b, done, :], ctlo[b, done, :]), NN)
            t = dot3(fs, split(t), NN)
            cthi[b, at, :], ctlo[b, at, :] = split(t)

        for b in range(5):
            col(b)
        for b in range(5, 8):
            @pl.when(use(b))
            def _():
                col(b)

    def update(lo, hi):
        at = slice(lo * H, hi * H)

        def tile(a, b):
            d = dot3((phi[a, :, at], plo[a, :, at]), (cthi[b, at, :], ctlo[b, at, :]), NN)
            if b == 0:
                d = jnp.where(z < 2, 0.0, d)
            tiles[a, b] = tiles[a, b] - d

        for b in range(5):
            tile(1, b)
        tile(0, 0)
        for n in range(1, 4):
            @pl.when(px >= n)
            def _():
                tile(1, 4 + n)
                tile(0, n)

    for s in range(4):
        @pl.when(jnp.logical_not(relay | root))
        def _():
            fac_wait(s)
            fac_spread(s, start)
        solve(s)
        if s == 1:
            update(0, 2)
        if s > 1:
            update(s, s + 1)

    for a in range(2):
        for b in range(8):
            @pl.when(r + 32 * a < z + 8 * b)
            def _():
                tiles[a, b] = jnp.zeros((NB, NB), F32)

    for p in range(2):
        @pl.when((z == p) & (r == p))
        def _():
            ri = lax.broadcasted_iota(jnp.int32, (NB, NB), 0)
            ci = lax.broadcasted_iota(jnp.int32, (NB, NB), 1)
            tiles[0, 0] = jnp.where(ri >= ci, tiles[0, 0], 0.0)

    @pl.when((r == 1) & (z == 0))
    def _():
        corner_send(0, (0, 0)).wait_send()

    @pl.when(extra)
    def _():
        corner_send(1, (0, 0)).wait_send()

    def sent(i, c):
        for p in range(2):
            @pl.when(i >= row_first[p])
            def _():
                row_spread(p, i, wait_send)
        for t in range(4):
            col_spread(t, i, wait_send)
        return c

    for b in range(8):
        give(b).wait_send()

    lax.fori_loop(0, NC, sent, 0)
    for s in range(4):
        fac_spread(s, wait_send)


def writer(t, o, buf, isem, osem):
    def get(a, b):
        return pltpu.make_async_copy(t.at[a, b], buf.at[a, b], isem.at[a, b])

    def put(a, b, h):
        return pltpu.make_async_copy(buf.at[a, b, :, pl.ds(h * H, H)], o.at[a, :, b, h, :], osem.at[a, b, h])

    which = [(a, b) for a in range(2) for b in range(8)]
    for w in which:
        get(*w).start()
    for w in which:
        get(*w).wait()
        for h in range(2):
            put(*w, h).start()
    for w in which:
        for h in range(2):
            put(*w, h).wait()


def on_device(trailing_in):
    x = trailing_in.reshape(2, NB, 8, 2, H)
    dma = pltpu.SemaphoreType.DMA
    t = pl.pallas_call(
        kernel,
        out_shape=jax.ShapeDtypeStruct((2, 8, NB, NB), F32),
        in_specs=[pl.BlockSpec(memory_space=pl.ANY)],
        out_specs=pl.BlockSpec(memory_space=pltpu.VMEM),
        scratch_shapes=[
            pltpu.VMEM((2, 8, NB, NB), F32),
            pltpu.VMEM((2, 2, NB, NB), F32),
            pltpu.VMEM((2, NB, NB), F32),
            pltpu.VMEM((10, H, H), F32),
            pltpu.VMEM((4, 4, H, H), F32),
            pltpu.VMEM((H, H), F32),
            pltpu.VMEM((2, NB, 2 * NB), BF),
            pltpu.VMEM((2, NB, 2 * NB), BF),
            pltpu.VMEM((8, 2 * NB, NB), BF),
            pltpu.VMEM((8, 2 * NB, NB), BF),
            dma((2, 8, 2)), dma((8, 2)), dma((2, 2)),
            dma((4, NC)), dma((8,)), dma((2, NC)), dma((2,)), dma((4,)),
            dma((4, 4, NC)), dma((8,)), dma((2, 2, NC)), dma((1,)),
            dma((4, 7)), dma((4, 3)), dma((4, 3)), dma((4,)),
        ],
        compiler_params=pltpu.CompilerParams(
            collective_id=0, has_side_effects=True, vmem_limit_bytes=56 << 20
        ),
    )(x)
    out = pl.pallas_call(
        writer,
        out_shape=jax.ShapeDtypeStruct(x.shape, F32),
        in_specs=[pl.BlockSpec(memory_space=pl.ANY)],
        out_specs=pl.BlockSpec(memory_space=pl.ANY),
        scratch_shapes=[pltpu.VMEM((2, 8, NB, NB), F32), dma((2, 8)), dma((2, 8, 2))],
        compiler_params=pltpu.CompilerParams(vmem_limit_bytes=56 << 20),
    )(t)
    return out.reshape(trailing_in.shape)


def solution(mesh):
    spec = P(None, "row", None, None, "col", None)
    return jax.shard_map(on_device, mesh=mesh, in_specs=(spec,), out_specs=spec, check_vma=False)
```

time: 796 us -> 76.3 us (0.10)
  the two profiles are of different devices: /device:TPU:77 before, /device:TPU:247 now
where the time goes in v2:
time: 76.3 us; the launch traced here: 76.2 us
  Pallas kernels  76 us (100%)
    pallas_call x1, Pallas kernels, on_device(): pl.pallas_call(kernel, out_shape=jax.ShapeDtypeStruct((2, 8, NB, NB), F32...  72 us
    pallas_call x1, Pallas kernels, on_device(): pl.pallas_call(writer, out_shape=jax.ShapeDtypeStruct(x.shape, F32), in_s...  3.99 us

profile of v2, /device:TPU:247, one launch (start us, length us, event | category | flops | bytes accessed | tf_op | source)
XLA Modules:
  0.0 76.2 jit_solution(10103335268750612812)
XLA Ops:
  0.0 72.0 %shard_map.17.t = f32[2,8,256,256]{3,2,1,0:T(8,128)} custom-call(f32[2,256,8,2,128]{4,3,2,1,0:T(2,128)} %bitcast.2), custom_call_target="tpu_custom_call" | custom-call | tf_op jit(solution)/shard_map/pallas_call | solution.py:549
  72.1 4.0 %shard_map.18 = f32[2,256,8,2,128]{4,3,2,1,0:T(2,128)} custom-call(f32[2,8,256,256]{3,2,1,0:T(8,128)} %shard_map.17.t), custom_call_target="tpu_custom_call" | custom-call | tf_op jit(solution)/shard_map/pallas_call | solution.py:574

commit v3 on v2

--- a/solution.py
+++ b/solution.py
@@ -117,15 +117,17 @@
 CH = 64
 NC = 2 * NB // CH
 PER = NB // CH
-HOP = 4
+HOP = 3
 DIRS = ((1, 0), (0, 1), (-1, 0), (0, -1))
 PARENT = {(1, 0): 0, (2, 0): 0, (1, 1): 1, (1, 3): 3, (2, 1): 0, (1, 2): 1, (0, 1): 2, (0, 3): 2,
           (3, 0): 0, (2, 3): 3, (2, 2): 0, (0, 2): 2, (3, 1): 0, (3, 3): 0, (3, 2): 0}
-FSTEP = (7, 10, 13, 16)
-FLEVEL = 3
-STEPS = NC + 5 * HOP
+QUARTERED = 0
+QSTEP = (0, 0)
+ZSTEP = (8, 10, 13, 16)
+FAR = 3
+STEPS = max(QSTEP[1] + 4 * HOP + 1, NC + 5 * HOP, ZSTEP[3] + 2 * FAR + 1)
 OTHER = (2, 1, 3)
-ZFAN = {0: (2, 6, 1, 7), 2: (4, 3), 6: (5,)}
+ZFAN = {0: (2, 6), 2: (4, 3, 1), 6: (5, 7)}
 
 
 def tree_tables():
@@ -146,6 +148,10 @@
 CHILD, DEPTH = tree_tables()
 
 
+WORK = tuple((1, b) for b in range(8)) + tuple((0, b) for b in range(4))
+UPPER = tuple((0, b) for b in range(4, 8))
+
+
 def bit(mask, n):
     hit = False
     for i in range(16):
@@ -154,8 +160,8 @@
     return hit
 
 
-def kernel(x, tiles, cols, rows, corner, fac, cm, linv, phi, plo, cthi, ctlo,
-           ld, ldc, ldr, colsem, givesem, rowsem, csem, fsem, scol, sgive, srow, sc, fz, fx, fy, fk):
+def kernel(x, o, tiles, cols, rows, corner, fac, cm, linv, phi, plo, cthi, ctlo, tchi, tclo, trhi, trlo,
+           ld, ldc, ldr, st, colsem, givesem, rowsem, csem, fsem, fq, scol, sgive, srow, sc, fz, fx, fy, fk, sq):
     r = lax.axis_index("row")
     z = lax.axis_index("col")
     px, py, k = r // 8, (r // 2) % 4, r % 2
@@ -185,10 +191,12 @@
             for h in range(2):
                 load_col(b, h).start()
 
-    for a in range(2):
-        for b in range(8):
-            for h in range(2):
-                load(a, b, h).start()
+    for a, b in WORK:
+        for h in range(2):
+            load(a, b, h).start()
+
+    def store(a, b):
+        return pltpu.make_async_copy(tiles.at[a, b], o.at[a, b], st.at[a, b])
 
     barrier = pltpu.get_barrier_semaphore()
 
@@ -251,7 +259,7 @@
 
     def row_send(p, i, d, zz):
         ref = rows.at[p, i // PER, pl.ds((i % PER) * CH, CH)]
-        return send(ref, srow.at[p, d, i], rowsem.at[p, i], (r, zz))
+        return send(ref, srow.at[p, d], rowsem.at[p, i], (r, zz))
 
     row_depth = (jnp.where(z < 3, z, 8 - z),
                  jnp.where(z == 0, 1, jnp.where((z == 7) & (r > 0), 2, z - 1)))
@@ -290,7 +298,7 @@
 
     def col_send(t, i, d, dev):
         ref = cols.at[k, t + 4 * (i // PER), pl.ds((i % PER) * CH, CH)]
-        return send(ref, scol.at[t, d, i], colsem.at[t, i], dev)
+        return send(ref, scol.at[t, d], colsem.at[t, i], dev)
 
     def col_spread(t, i, act):
         for d in range(4):
@@ -324,13 +332,14 @@
         ref = fac.at[pl.ds(STAGE[s], STAGE[s + 1] - STAGE[s])]
         return send(ref, ss, fsem.at[s], dev)
 
-    def fac_spread(s, act):
+    def z_spread(s, act):
         for at, to in ZFAN.items():
             @pl.when((r == 0) & (z == at))
             def _():
                 for d in to:
                     act(fac_send(s, fz.at[s, d - 1], (0, d)))
 
+    def xy_spread(s, act):
         @pl.when(r == 0)
         def _():
             for n in range(3):
@@ -341,15 +350,43 @@
             for n in range(3):
                 act(fac_send(s, fy.at[s, n], (px * 8 + OTHER[n] * 2, z)))
 
+    def k_spread(s, act):
         @pl.when(k == 0)
         def _():
             act(fac_send(s, fk.at[s], partner))
+
+    def quarter(s, t, d, dev):
+        ref = fac.at[pl.ds(STAGE[s], STAGE[s + 1] - STAGE[s]), pl.ds(t * 32, 32)]
+        return send(ref, sq.at[s, t, d], fq.at[s, t], dev)
+
+    def q_spread(s, t, act):
+        for d in range(4):
+            dx, dy = DIRS[(d + t) % 4]
+
+            @pl.when(links[t][d] & (k == 0))
+            def _():
+                act(quarter(s, t, d, (((px + dx + 4) % 4) * 8 + ((py + dy + 4) % 4) * 2, z)))
+
+    def fac_spread(s, act):
+        z_spread(s, act)
+        if s < QUARTERED:
+            for t in range(4):
+                q_spread(s, t, act)
+        else:
+            xy_spread(s, act)
+        k_spread(s, act)
 
     def fac_wait(s):
         fac_send(s, fk.at[s], partner).wait_recv()
 
-    relay = (k == 0) & (py == 0) & jnp.logical_not(root)
-    level = (jnp.where((z > 2) & (z < 6), 1, 0) + jnp.where(px > 0, 1, 0)) * FLEVEL
+    hub = (r == 0) & (z > 0)
+    relay = (k == 0) & (py == 0) & (px > 0)
+    inner = (k == 0) & (r > 0)
+    far = jnp.where((z == 2) | (z == 6) | (z == 0), 0, FAR)
+    kids = [ln[0] | ln[1] | ln[2] | ln[3] for ln in links]
+
+    def quarter_wait(s, t):
+        quarter(s, t, 0, partner).wait_recv()
 
     @pl.when((r == 1) & (z == 0))
     def _():
@@ -370,14 +407,40 @@
             row_step(p, step)
         for t in range(4):
             col_step(t, step)
-        for s in range(4):
-            @pl.when(relay & (step == FSTEP[s] + level))
-            def _():
-                fac_wait(s)
-                fac_spread(s, start)
+        @pl.when(hub)
+        def _():
+            for s in range(4):
+                @pl.when(step == ZSTEP[s] + far)
+                def _():
+                    fac_wait(s)
+                    z_spread(s, start)
+                    if s >= QUARTERED:
+                        xy_spread(s, start)
+                    k_spread(s, start)
+
+        @pl.when(relay)
+        def _():
+            for s in range(QUARTERED, 4):
+                @pl.when(step == ZSTEP[s] + far + FAR)
+                def _():
+                    fac_wait(s)
+                    xy_spread(s, start)
+                    k_spread(s, start)
+
+        if QUARTERED:
+            @pl.when((hub | inner) & (step >= QSTEP[0]))
+            def _():
+                for t in range(4):
+                    for s in range(QUARTERED):
+                        @pl.when((step == QSTEP[s] + frames[t]) & kids[t])
+                        def _():
+                            @pl.when(inner)
+                            def _():
+                                quarter_wait(s, t)
+                            q_spread(s, t, start)
         return c
 
-    lax.fori_loop(0, jnp.where(root, NC, jnp.where((r == 0) & (z > 5), STEPS + HOP, STEPS)), step_body, 0)
+    lax.fori_loop(0, jnp.where(root, NC, STEPS), step_body, 0)
 
     @pl.when(root)
     def _():
@@ -415,26 +478,45 @@
                 return c
             lax.fori_loop(row_first[p], NC, body, 0)
 
+    for a, b in UPPER:
+        tiles[a, b] = jnp.zeros((NB, NB), F32)
+        store(a, b).start()
+
+    @pl.when(inner)
+    def _():
+        for s in range(QUARTERED):
+            for t in range(4):
+                @pl.when(jnp.logical_not(kids[t]))
+                def _():
+                    quarter_wait(s, t)
+            k_spread(s, start)
+
     for b in range(8):
         give(b).wait_recv()
 
-    for a in range(2):
+    for a, b in WORK:
+        for h in range(2):
+            load(a, b, h).wait()
+
+    def lefts(s):
+        return split(jnp.concatenate([fac[blk(s, m)] for m in range(s)], axis=1))
+
+    def prepare(s):
+        w = (s % 2) * H
+        done = slice(0, s * H)
+        fl = lefts(s)
+        for a in range(2):
+            trhi[a], trlo[a] = split(rows[s // 2, a, :, w:w + H] - dot3((phi[a, :, done], plo[a, :, done]), fl, NT))
         for b in range(8):
-            for h in range(2):
-                load(a, b, h).wait()
+            tchi[b], tclo[b] = split(cols[s // 2, b, w:w + H, :] - dot3(fl, (cthi[b, done, :], ctlo[b, done, :]), NN))
 
     def solve(s):
         w = (s % 2) * H
         at = slice(s * H, (s + 1) * H)
-        done = slice(0, s * H)
         fs = split(fac[blk(s, s)])
-        if s:
-            fl = split(jnp.concatenate([fac[blk(s, m)] for m in range(s)], axis=1))
         for a in range(2):
-            t = rows[s // 2, a, :, w:w + H]
-            if s:
-                t = t - dot3((phi[a, :, done], plo[a, :, done]), fl, NT)
-            t = dot3(split(t), fs, NT)
+            t = (trhi[a], trlo[a]) if s else split(rows[0, a, :, :H])
+            t = dot3(t, fs, NT)
             phi[a, :, at], plo[a, :, at] = split(t)
 
             @pl.when((z == s // 2) & (r + 32 * a >= z))
@@ -442,86 +524,70 @@
                 if w == 0:
                     tiles[a, 0, :, H:] = jnp.zeros((NB, H), F32)
                 tiles[a, 0, :, w:w + H] = t
-
-        def col(b):
-            t = cols[s // 2, b, w:w + H, :]
-            if s:
-                t = t - dot3(fl, (cthi[b, done, :], ctlo[b, done, :]), NN)
-            t = dot3(fs, split(t), NN)
-            cthi[b, at, :], ctlo[b, at, :] = split(t)
-
-        for b in range(5):
-            col(b)
-        for b in range(5, 8):
-            @pl.when(use(b))
-            def _():
-                col(b)
-
-    def update(lo, hi):
+        for b in range(8):
+            t = (tchi[b], tclo[b]) if s else split(cols[0, b, :H, :])
+            cthi[b, at, :], ctlo[b, at, :] = split(dot3(fs, t, NN))
+
+    ri = lax.broadcasted_iota(jnp.int32, (NB, NB), 0)
+    ci = lax.broadcasted_iota(jnp.int32, (NB, NB), 1)
+
+    def update(lo, hi, last):
         at = slice(lo * H, hi * H)
-
-        def tile(a, b):
+        for a, b in WORK:
             d = dot3((phi[a, :, at], plo[a, :, at]), (cthi[b, at, :], ctlo[b, at, :]), NN)
             if b == 0:
                 d = jnp.where(z < 2, 0.0, d)
-            tiles[a, b] = tiles[a, b] - d
-
-        for b in range(5):
-            tile(1, b)
-        tile(0, 0)
-        for n in range(1, 4):
-            @pl.when(px >= n)
-            def _():
-                tile(1, 4 + n)
-                tile(0, n)
+            d = tiles[a, b] - d
+            if last:
+                keep = r + 32 * a >= z + 8 * b
+                if (a, b) == (0, 0):
+                    keep = keep & ((ri >= ci) | (z > 1) | (r != z))
+                d = jnp.where(keep, d, 0.0)
+            tiles[a, b] = d
+            if last:
+                store(a, b).start()
 
     for s in range(4):
-        @pl.when(jnp.logical_not(relay | root))
+        @pl.when((k == 1) | (inner & (s >= QUARTERED) & jnp.logical_not(relay)))
         def _():
             fac_wait(s)
-            fac_spread(s, start)
+            if s >= QUARTERED:
+                k_spread(s, start)
         solve(s)
         if s == 1:
-            update(0, 2)
-        if s > 1:
-            update(s, s + 1)
-
-    for a in range(2):
-        for b in range(8):
-            @pl.when(r + 32 * a < z + 8 * b)
-            def _():
-                tiles[a, b] = jnp.zeros((NB, NB), F32)
+            update(0, 2, False)
+        if s < 3:
+            prepare(s + 1)
+    update(2, 4, True)
+
+    @pl.when((r == 1) & (z == 0))
+    def _():
+        corner_send(0, (0, 0)).wait_send()
+
+    @pl.when(extra)
+    def _():
+        corner_send(1, (0, 0)).wait_send()
 
     for p in range(2):
-        @pl.when((z == p) & (r == p))
-        def _():
-            ri = lax.broadcasted_iota(jnp.int32, (NB, NB), 0)
-            ci = lax.broadcasted_iota(jnp.int32, (NB, NB), 1)
-            tiles[0, 0] = jnp.where(ri >= ci, tiles[0, 0], 0.0)
-
-    @pl.when((r == 1) & (z == 0))
-    def _():
-        corner_send(0, (0, 0)).wait_send()
-
-    @pl.when(extra)
-    def _():
-        corner_send(1, (0, 0)).wait_send()
-
-    def sent(i, c):
-        for p in range(2):
-            @pl.when(i >= row_first[p])
-            def _():
-                row_spread(p, i, wait_send)
-        for t in range(4):
-            col_spread(t, i, wait_send)
-        return c
-
+        for d, on in ((0, row_down[p]), (1, row_up[p])):
+            @pl.when(on & (row_first[p] == 0))
+            def _():
+                send(rows.at[p], srow.at[p, d], rowsem.at[p, 0], partner).wait_send()
+
+            @pl.when(on & (row_first[p] > 0))
+            def _():
+                send(rows.at[p, 1], srow.at[p, d], rowsem.at[p, 0], partner).wait_send()
+    for t in range(4):
+        for d in range(4):
+            @pl.when(links[t][d])
+            def _():
+                send(cols.at[k, pl.ds(0, 2)], scol.at[t, d], colsem.at[t, 0], partner).wait_send()
     for b in range(8):
         give(b).wait_send()
-
-    lax.fori_loop(0, NC, sent, 0)
     for s in range(4):
         fac_spread(s, wait_send)
+    for a, b in WORK + UPPER:
+        store(a, b).wait()
 
 
 def writer(t, o, buf, isem, osem):
@@ -550,8 +616,9 @@
         kernel,
         out_shape=jax.ShapeDtypeStruct((2, 8, NB, NB), F32),
         in_specs=[pl.BlockSpec(memory_space=pl.ANY)],
-        out_specs=pl.BlockSpec(memory_space=pltpu.VMEM),
+        out_specs=pl.BlockSpec(memory_space=pl.ANY),
         scratch_shapes=[
+            pltpu.VMEM((2, 8, NB, NB), F32),
             pltpu.VMEM((2, 8, NB, NB), F32),
             pltpu.VMEM((2, 2, NB, NB), F32),
             pltpu.VMEM((2, NB, NB), F32),
@@ -562,10 +629,14 @@
             pltpu.VMEM((2, NB, 2 * NB), BF),
             pltpu.VMEM((8, 2 * NB, NB), BF),
             pltpu.VMEM((8, 2 * NB, NB), BF),
-            dma((2, 8, 2)), dma((8, 2)), dma((2, 2)),
-            dma((4, NC)), dma((8,)), dma((2, NC)), dma((2,)), dma((4,)),
-            dma((4, 4, NC)), dma((8,)), dma((2, 2, NC)), dma((1,)),
-            dma((4, 7)), dma((4, 3)), dma((4, 3)), dma((4,)),
+            pltpu.VMEM((8, H, NB), BF),
+            pltpu.VMEM((8, H, NB), BF),
+            pltpu.VMEM((2, NB, H), BF),
+            pltpu.VMEM((2, NB, H), BF),
+            dma((2, 8, 2)), dma((8, 2)), dma((2, 2)), dma((2, 8)),
+            dma((4, NC)), dma((8,)), dma((2, NC)), dma((2,)), dma((4,)), dma((2, 4)),
+            dma((4, 4)), dma((8,)), dma((2, 2)), dma((1,)),
+            dma((4, 7)), dma((4, 3)), dma((4, 3)), dma((4,)), dma((2, 4, 4)),
         ],
         compiler_params=pltpu.CompilerParams(
             collective_id=0, has_side_effects=True, vmem_limit_bytes=56 << 20

time: 76.3 us -> 61 us (0.80)
  the two profiles are of different devices: /device:TPU:247 before, /device:TPU:77 now
where the time goes in v3:
time: 61 us; the launch traced here: 59.9 us
  Pallas kernels  59.7 us (98%)
    pallas_call x1, Pallas kernels, on_device(): pl.pallas_call(kernel, out_shape=jax.ShapeDtypeStruct((2, 8, NB, NB), F32...  55.7 us
    pallas_call x1, Pallas kernels, on_device(): pl.pallas_call(writer, out_shape=jax.ShapeDtypeStruct(x.shape, F32), in_s...  3.99 us

profile of v3, /device:TPU:77, one launch (start us, length us, event | category | flops | bytes accessed | tf_op | source)
XLA Modules:
  0.0 59.9 jit_solution(6832825193744979426)
XLA Ops:
  0.0 55.7 %shard_map.17.t = f32[2,8,256,256]{3,2,1,0:T(8,128)} custom-call(f32[2,256,8,2,128]{4,3,2,1,0:T(2,128)} %bitcast.2), custom_call_target="tpu_custom_call" | custom-call | tf_op jit(solution)/shard_map/pallas_call | solution.py:615
  55.7 4.0 %shard_map.18 = f32[2,256,8,2,128]{4,3,2,1,0:T(2,128)} custom-call(f32[2,8,256,256]{3,2,1,0:T(8,128)} %shard_map.17.t), custom_call_target="tpu_custom_call" | custom-call | tf_op jit(solution)/shard_map/pallas_call | solution.py:645

commit v4 on v3

--- a/solution.py
+++ b/solution.py
@@ -110,6 +110,10 @@
     return g(a[0], b[0]) + (g(a[0], b[1]) + g(a[1], b[0]))
 
 
+def dot_nn(a, b):
+    return lax.dot_general(a, b, NN, precision=HI, preferred_element_type=F32)
+
+
 def dot_hi(a, b):
     return lax.dot_general(a, b, NT, precision=HI, preferred_element_type=F32)
 
@@ -121,11 +125,9 @@
 DIRS = ((1, 0), (0, 1), (-1, 0), (0, -1))
 PARENT = {(1, 0): 0, (2, 0): 0, (1, 1): 1, (1, 3): 3, (2, 1): 0, (1, 2): 1, (0, 1): 2, (0, 3): 2,
           (3, 0): 0, (2, 3): 3, (2, 2): 0, (0, 2): 2, (3, 1): 0, (3, 3): 0, (3, 2): 0}
-QUARTERED = 0
-QSTEP = (0, 0)
 ZSTEP = (8, 10, 13, 16)
 FAR = 3
-STEPS = max(QSTEP[1] + 4 * HOP + 1, NC + 5 * HOP, ZSTEP[3] + 2 * FAR + 1)
+STEPS = max(NC + 5 * HOP, ZSTEP[3] + 2 * FAR + 1)
 OTHER = (2, 1, 3)
 ZFAN = {0: (2, 6), 2: (4, 3, 1), 6: (5, 7)}
 
@@ -161,7 +163,7 @@
 
 
 def kernel(x, o, tiles, cols, rows, corner, fac, cm, linv, phi, plo, cthi, ctlo, tchi, tclo, trhi, trlo,
-           ld, ldc, ldr, st, colsem, givesem, rowsem, csem, fsem, fq, scol, sgive, srow, sc, fz, fx, fy, fk, sq):
+           ld, ldc, ldr, st, colsem, givesem, rowsem, csem, fsem, scol, sgive, srow, sc, fz, fx, fy, fk):
     r = lax.axis_index("row")
     z = lax.axis_index("col")
     px, py, k = r // 8, (r // 2) % 4, r % 2
@@ -328,66 +330,51 @@
     def use(b):
         return px >= b - 4
 
-    def fac_send(s, ss, dev):
-        ref = fac.at[pl.ds(STAGE[s], STAGE[s + 1] - STAGE[s])]
-        return send(ref, ss, fsem.at[s], dev)
-
-    def z_spread(s, act):
+    def fac_send(j, ss, dev):
+        return send(fac.at[j], ss, fsem.at[j], dev)
+
+    def z_spread(js, act):
         for at, to in ZFAN.items():
             @pl.when((r == 0) & (z == at))
             def _():
-                for d in to:
-                    act(fac_send(s, fz.at[s, d - 1], (0, d)))
-
-    def xy_spread(s, act):
+                for j in js:
+                    for d in to:
+                        act(fac_send(j, fz.at[j, d - 1], (0, d)))
+
+    def xy_spread(js, act):
         @pl.when(r == 0)
         def _():
-            for n in range(3):
-                act(fac_send(s, fx.at[s, n], (OTHER[n] * 8, z)))
+            for j in js:
+                for n in range(3):
+                    act(fac_send(j, fx.at[j, n], (OTHER[n] * 8, z)))
 
         @pl.when((py == 0) & (k == 0))
         def _():
-            for n in range(3):
-                act(fac_send(s, fy.at[s, n], (px * 8 + OTHER[n] * 2, z)))
-
-    def k_spread(s, act):
+            for j in js:
+                for n in range(3):
+                    act(fac_send(j, fy.at[j, n], (px * 8 + OTHER[n] * 2, z)))
+
+    def k_spread(js, act):
         @pl.when(k == 0)
         def _():
-            act(fac_send(s, fk.at[s], partner))
-
-    def quarter(s, t, d, dev):
-        ref = fac.at[pl.ds(STAGE[s], STAGE[s + 1] - STAGE[s]), pl.ds(t * 32, 32)]
-        return send(ref, sq.at[s, t, d], fq.at[s, t], dev)
-
-    def q_spread(s, t, act):
-        for d in range(4):
-            dx, dy = DIRS[(d + t) % 4]
-
-            @pl.when(links[t][d] & (k == 0))
-            def _():
-                act(quarter(s, t, d, (((px + dx + 4) % 4) * 8 + ((py + dy + 4) % 4) * 2, z)))
-
-    def fac_spread(s, act):
-        z_spread(s, act)
-        if s < QUARTERED:
-            for t in range(4):
-                q_spread(s, t, act)
-        else:
-            xy_spread(s, act)
-        k_spread(s, act)
-
-    def fac_wait(s):
-        fac_send(s, fk.at[s], partner).wait_recv()
+            for j in js:
+                act(fac_send(j, fk.at[j], partner))
+
+    def fac_spread(js, act):
+        z_spread(js, act)
+        xy_spread(js, act)
+        k_spread(js, act)
+
+    def fac_wait(j):
+        fac_send(j, fk.at[j], partner).wait_recv()
+
+    def blocks(s):
+        return range(STAGE[s], STAGE[s + 1])
 
     hub = (r == 0) & (z > 0)
     relay = (k == 0) & (py == 0) & (px > 0)
     inner = (k == 0) & (r > 0)
     far = jnp.where((z == 2) | (z == 6) | (z == 0), 0, FAR)
-    kids = [ln[0] | ln[1] | ln[2] | ln[3] for ln in links]
-
-    def quarter_wait(s, t):
-        quarter(s, t, 0, partner).wait_recv()
-
     @pl.when((r == 1) & (z == 0))
     def _():
         corner_send(0, (0, 0)).start()
@@ -412,32 +399,20 @@
             for s in range(4):
                 @pl.when(step == ZSTEP[s] + far)
                 def _():
-                    fac_wait(s)
-                    z_spread(s, start)
-                    if s >= QUARTERED:
-                        xy_spread(s, start)
-                    k_spread(s, start)
+                    for j in blocks(s):
+                        fac_wait(j)
+                        fac_spread([j], start)
 
         @pl.when(relay)
         def _():
-            for s in range(QUARTERED, 4):
+            for s in range(4):
                 @pl.when(step == ZSTEP[s] + far + FAR)
                 def _():
-                    fac_wait(s)
-                    xy_spread(s, start)
-                    k_spread(s, start)
-
-        if QUARTERED:
-            @pl.when((hub | inner) & (step >= QSTEP[0]))
-            def _():
-                for t in range(4):
-                    for s in range(QUARTERED):
-                        @pl.when((step == QSTEP[s] + frames[t]) & kids[t])
-                        def _():
-                            @pl.when(inner)
-                            def _():
-                                quarter_wait(s, t)
-                            q_spread(s, t, start)
+                    for j in blocks(s):
+                        fac_wait(j)
+                        xy_spread([j], start)
+                        k_spread([j], start)
+
         return c
 
     lax.fori_loop(0, jnp.where(root, NC, STEPS), step_body, 0)
@@ -460,9 +435,10 @@
                 @pl.when(t == s)
                 def _():
                     fac[blk(s, s)] = linv[...]
+                    fac_spread([blk(s, s)], start)
                     for i in range(s + 1, 4):
                         fac[blk(i, s)] = dot_hi(cm[i, s], linv[...])
-                    fac_spread(s, start)
+                        fac_spread([blk(i, s)], start)
                     for i in range(s + 1, 4):
                         for j in range(s + 1, i + 1):
                             cm[i, j] = cm[i, j] - dot_hi(fac[blk(i, s)], fac[blk(j, s)])
@@ -478,19 +454,6 @@
                 return c
             lax.fori_loop(row_first[p], NC, body, 0)
 
-    for a, b in UPPER:
-        tiles[a, b] = jnp.zeros((NB, NB), F32)
-        store(a, b).start()
-
-    @pl.when(inner)
-    def _():
-        for s in range(QUARTERED):
-            for t in range(4):
-                @pl.when(jnp.logical_not(kids[t]))
-                def _():
-                    quarter_wait(s, t)
-            k_spread(s, start)
-
     for b in range(8):
         give(b).wait_recv()
 
@@ -498,35 +461,33 @@
         for h in range(2):
             load(a, b, h).wait()
 
-    def lefts(s):
-        return split(jnp.concatenate([fac[blk(s, m)] for m in range(s)], axis=1))
-
-    def prepare(s):
-        w = (s % 2) * H
-        done = slice(0, s * H)
-        fl = lefts(s)
+    def inverse(p):
+        lo, hi = 2 * p, 2 * p + 1
+        a, b = fac[blk(lo, lo)], fac[blk(hi, hi)]
+        m = dot_nn(dot_nn(b, fac[blk(hi, lo)]), a)
+        top = jnp.concatenate([a, jnp.zeros((H, H), F32)], axis=1)
+        return split(jnp.concatenate([top, jnp.concatenate([-m, b], axis=1)], axis=0))
+
+    def prepare():
+        left = split(jnp.concatenate([jnp.concatenate([fac[blk(i, m)] for m in range(2)], axis=1) for i in (2, 3)], axis=0))
         for a in range(2):
-            trhi[a], trlo[a] = split(rows[s // 2, a, :, w:w + H] - dot3((phi[a, :, done], plo[a, :, done]), fl, NT))
+            trhi[a], trlo[a] = split(rows[1, a] - dot3((phi[a, :, :NB], plo[a, :, :NB]), left, NT))
         for b in range(8):
-            tchi[b], tclo[b] = split(cols[s // 2, b, w:w + H, :] - dot3(fl, (cthi[b, done, :], ctlo[b, done, :]), NN))
-
-    def solve(s):
-        w = (s % 2) * H
-        at = slice(s * H, (s + 1) * H)
-        fs = split(fac[blk(s, s)])
+            tchi[b], tclo[b] = split(cols[1, b] - dot3(left, (cthi[b, :NB, :], ctlo[b, :NB, :]), NN))
+
+    def solve(p):
+        at = slice(p * NB, (p + 1) * NB)
+        inv = inverse(p)
         for a in range(2):
-            t = (trhi[a], trlo[a]) if s else split(rows[0, a, :, :H])
-            t = dot3(t, fs, NT)
+            t = dot3((trhi[a], trlo[a]) if p else split(rows[0, a]), inv, NT)
             phi[a, :, at], plo[a, :, at] = split(t)
 
-            @pl.when((z == s // 2) & (r + 32 * a >= z))
-            def _():
-                if w == 0:
-                    tiles[a, 0, :, H:] = jnp.zeros((NB, H), F32)
-                tiles[a, 0, :, w:w + H] = t
+            @pl.when((z == p) & (r + 32 * a >= z))
+            def _():
+                tiles[a, 0] = t
         for b in range(8):
-            t = (tchi[b], tclo[b]) if s else split(cols[0, b, :H, :])
-            cthi[b, at, :], ctlo[b, at, :] = split(dot3(fs, t, NN))
+            t = (tchi[b], tclo[b]) if p else split(cols[0, b])
+            cthi[b, at, :], ctlo[b, at, :] = split(dot3(inv, t, NN))
 
     ri = lax.broadcasted_iota(jnp.int32, (NB, NB), 0)
     ci = lax.broadcasted_iota(jnp.int32, (NB, NB), 1)
@@ -547,17 +508,21 @@
             if last:
                 store(a, b).start()
 
-    for s in range(4):
-        @pl.when((k == 1) | (inner & (s >= QUARTERED) & jnp.logical_not(relay)))
-        def _():
-            fac_wait(s)
-            if s >= QUARTERED:
-                k_spread(s, start)
-        solve(s)
-        if s == 1:
-            update(0, 2, False)
-        if s < 3:
-            prepare(s + 1)
+    def arrive(s):
+        @pl.when((k == 1) | (inner & jnp.logical_not(relay)))
+        def _():
+            for j in blocks(s):
+                fac_wait(j)
+                k_spread([j], start)
+
+    arrive(0)
+    arrive(1)
+    solve(0)
+    update(0, 2, False)
+    prepare()
+    arrive(2)
+    arrive(3)
+    solve(1)
     update(2, 4, True)
 
     @pl.when((r == 1) & (z == 0))
@@ -584,9 +549,8 @@
                 send(cols.at[k, pl.ds(0, 2)], scol.at[t, d], colsem.at[t, 0], partner).wait_send()
     for b in range(8):
         give(b).wait_send()
-    for s in range(4):
-        fac_spread(s, wait_send)
-    for a, b in WORK + UPPER:
+    fac_spread(range(10), wait_send)
+    for a, b in WORK:
         store(a, b).wait()
 
 
@@ -597,14 +561,17 @@
     def put(a, b, h):
         return pltpu.make_async_copy(buf.at[a, b, :, pl.ds(h * H, H)], o.at[a, :, b, h, :], osem.at[a, b, h])
 
-    which = [(a, b) for a in range(2) for b in range(8)]
-    for w in which:
+    for w in WORK:
         get(*w).start()
-    for w in which:
+    for a, b in UPPER:
+        buf[a, b] = jnp.zeros((NB, NB), F32)
+        for h in range(2):
+            put(a, b, h).start()
+    for w in WORK:
         get(*w).wait()
         for h in range(2):
             put(*w, h).start()
-    for w in which:
+    for w in WORK + UPPER:
         for h in range(2):
             put(*w, h).wait()
 
@@ -629,14 +596,14 @@
             pltpu.VMEM((2, NB, 2 * NB), BF),
             pltpu.VMEM((8, 2 * NB, NB), BF),
             pltpu.VMEM((8, 2 * NB, NB), BF),
-            pltpu.VMEM((8, H, NB), BF),
-            pltpu.VMEM((8, H, NB), BF),
-            pltpu.VMEM((2, NB, H), BF),
-            pltpu.VMEM((2, NB, H), BF),
+            pltpu.VMEM((8, NB, NB), BF),
+            pltpu.VMEM((8, NB, NB), BF),
+            pltpu.VMEM((2, NB, NB), BF),
+            pltpu.VMEM((2, NB, NB), BF),
             dma((2, 8, 2)), dma((8, 2)), dma((2, 2)), dma((2, 8)),
-            dma((4, NC)), dma((8,)), dma((2, NC)), dma((2,)), dma((4,)), dma((2, 4)),
+            dma((4, NC)), dma((8,)), dma((2, NC)), dma((2,)), dma((10,)),
             dma((4, 4)), dma((8,)), dma((2, 2)), dma((1,)),
-            dma((4, 7)), dma((4, 3)), dma((4, 3)), dma((4,)), dma((2, 4, 4)),
+            dma((10, 7)), dma((10, 3)), dma((10, 3)), dma((10,)),
         ],
         compiler_params=pltpu.CompilerParams(
             collective_id=0, has_side_effects=True, vmem_limit_bytes=56 << 20

time: 61 us -> 58.9 us (0.966); the launches traced: 59.9 us -> 58.8 us
  Pallas kernels: 59.7 us -> 58.6 us
    pallas_call x1, Pallas kernels: 55.7 us -> 55.1 us  [on_device(): pl.pallas_call(kernel, out_shape=jax.ShapeDtypeStruct((2, 8, NB, NB), F32...]
where the time goes in v4:
time: 58.9 us; the launch traced here: 58.8 us
  Pallas kernels  58.6 us (99%)
    pallas_call x1, Pallas kernels, on_device(): pl.pallas_call(kernel, out_shape=jax.ShapeDtypeStruct((2, 8, NB, NB), F32...  55.1 us
    pallas_call x1, Pallas kernels, on_device(): pl.pallas_call(writer, out_shape=jax.ShapeDtypeStruct(x.shape, F32), in_s...  3.54 us

profile of v4, /device:TPU:77, one launch (start us, length us, event | category | flops | bytes accessed | tf_op | source)
XLA Modules:
  0.0 58.8 jit_solution(15338628140167890636)
XLA Ops:
  0.0 55.1 %shard_map.17.t = f32[2,8,256,256]{3,2,1,0:T(8,128)} custom-call(f32[2,256,8,2,128]{4,3,2,1,0:T(2,128)} %bitcast.2), custom_call_target="tpu_custom_call" | custom-call | tf_op jit(solution)/shard_map/pallas_call | solution.py:582
  55.1 3.5 %shard_map.18 = f32[2,256,8,2,128]{4,3,2,1,0:T(2,128)} custom-call(f32[2,8,256,256]{3,2,1,0:T(8,128)} %shard_map.17.t), custom_call_target="tpu_custom_call" | custom-call | tf_op jit(solution)/shard_map/pallas_call | solution.py:612

commit v5 on v4

--- a/solution.py
+++ b/solution.py
@@ -446,6 +446,18 @@
 
         lax.fori_loop(0, 4, stage, 0)
 
+    pass_on = inner & jnp.logical_not(relay)
+
+    def arrive(s, who):
+        @pl.when(who)
+        def _():
+            for j in blocks(s):
+                fac_wait(j)
+                k_spread([j], start)
+
+    for s in range(3):
+        arrive(s, (k == 1) | pass_on)
+
     for p in range(2):
         @pl.when(row_from[p] & jnp.logical_not(row_down[p] | row_up[p]))
         def _():
@@ -508,20 +520,11 @@
             if last:
                 store(a, b).start()
 
-    def arrive(s):
-        @pl.when((k == 1) | (inner & jnp.logical_not(relay)))
-        def _():
-            for j in blocks(s):
-                fac_wait(j)
-                k_spread([j], start)
-
-    arrive(0)
-    arrive(1)
     solve(0)
+    arrive(3, pass_on)
     update(0, 2, False)
     prepare()
-    arrive(2)
-    arrive(3)
+    arrive(3, k == 1)
     solve(1)
     update(2, 4, True)
 

time: 58.9 us -> 60.3 us (1.024); the launches traced: 58.8 us -> 59.2 us
  no operation moved by 1% of the time
where the time goes in v5:
time: 60.3 us; the launch traced here: 59.2 us
  Pallas kernels  59 us (98%)
    pallas_call x1, Pallas kernels, on_device(): pl.pallas_call(kernel, out_shape=jax.ShapeDtypeStruct((2, 8, NB, NB), F32...  55.5 us
    pallas_call x1, Pallas kernels, on_device(): pl.pallas_call(writer, out_shape=jax.ShapeDtypeStruct(x.shape, F32), in_s...  3.54 us

profile of v5, /device:TPU:77, one launch (start us, length us, event | category | flops | bytes accessed | tf_op | source)
XLA Modules:
  0.0 59.2 jit_solution(5984973903210273219)
XLA Ops:
  0.0 55.5 %shard_map.17.t = f32[2,8,256,256]{3,2,1,0:T(8,128)} custom-call(f32[2,256,8,2,128]{4,3,2,1,0:T(2,128)} %bitcast.2), custom_call_target="tpu_custom_call" | custom-call | tf_op jit(solution)/shard_map/pallas_call | solution.py:585
  55.5 3.5 %shard_map.18 = f32[2,256,8,2,128]{4,3,2,1,0:T(2,128)} custom-call(f32[2,8,256,256]{3,2,1,0:T(8,128)} %shard_map.17.t), custom_call_target="tpu_custom_call" | custom-call | tf_op jit(solution)/shard_map/pallas_call | solution.py:615
